TPU v7x, 32 devices: a whole 2x2x4 slice. The times are simulated.
32 devices in a mesh: rows: 4 (over z), cols: 8 (over y, x, core).
Axes of the slice: x: 2, y: 2, z: 4, core: 2. Of those that a mesh axis runs over, the one named last changes fastest.
Arguments:
- whitened: float32 [3, 131072], P(None, ('rows', 'cols')), may hold values from -6 to 6
- cotangent: bfloat16 [64, 131072], P(None, ('rows', 'cols')), may hold values from -6 to 6
- lift_weight: float32 [64, 3], replicated, may hold values from -3.5 to 3.5
- conv_now: bfloat16 [3, 128, 64], replicated, may hold values from -0.5 to 0.5
- conv_past: bfloat16 [3, 128, 64], replicated, may hold values from -0.5 to 0.5
- mix_weight: bfloat16 [3, 64, 64], replicated, may hold values from -0.75 to 0.75
- dilations: int32 [3], replicated, may hold values from 64 to 256, as said below
- psd_bin: int32 [4096, 8, 4], P(None, 'cols', 'rows'), may hold values from 0 to 1023, as said below
- psd_weight: float32 [2, 1024], replicated, may hold values from 0.2 to 5
Outputs:
- data_grad: float32 [3, 131072], P(None, ('rows', 'cols'))
- grad_now: float32 [3, 128, 64], replicated
- grad_past: float32 [3, 128, 64], replicated
- grad_mix: float32 [3, 64, 64], replicated
- grad_lift: float32 [64, 3], replicated
Inputs may be any that keep to these rules, and one draw needn't show every extreme that they name: `dilations`: multiples of 4; one layer has 64, one has 256. `psd_bin`: frequencies k and 131072 - k have the same bin.
All inputs are finite; a program needn't handle non-finite values.
Results may differ from a plain program's by a relative error of at most 0.0068.
Values may be sent and summed in bfloat16 or wider, within the bound.
A program may use at most 64 MiB of HBM per device.

v0:
```python
import math

import jax
import jax.numpy as jnp
import numpy as np
from jax import lax
from jax.experimental import pallas as pl
from jax.experimental.pallas import tpu as pltpu
from jax.sharding import PartitionSpec as P

DMAX = 256
TILE = 128
MARGIN = 640
FRONT = 384
F32 = jnp.float32
BF16 = jnp.bfloat16


def halves(matrix):
    high = matrix.astype(np.float32).astype(jnp.bfloat16)
    low = (matrix - high.astype(np.float64)).astype(np.float32).astype(jnp.bfloat16)
    return np.stack([high, low])


def split(values):
    high = values.astype(BF16)
    return high, (values - high.astype(F32)).astype(BF16)


def dot_left(pair_ref, values):
    high, low = split(values)
    total = jnp.dot(pair_ref[0], high, preferred_element_type=F32)
    total += jnp.dot(pair_ref[0], low, preferred_element_type=F32)
    return total + jnp.dot(pair_ref[1], high, preferred_element_type=F32)


def dot_right(values, pair_ref):
    high, low = split(values)
    total = jnp.dot(high, pair_ref[0], preferred_element_type=F32)
    total += jnp.dot(low, pair_ref[0], preferred_element_type=F32)
    return total + jnp.dot(high, pair_ref[1], preferred_element_type=F32)


def chunks_of(first, last, size=1024):
    cuts = sorted({first, last} | {x for x in range(0, last, size) if first < x < last})
    return list(zip(cuts[:-1], cuts[1:]))


def layers_kernel(
    dil_ref, white_ref, left_ref, right_ref, cot_ref, cot_right_ref, lift_ref, now_ref, past_ref,
    mix_ref, bins_ref, psd_ref,
    dinput_ref, grads_ref, factor_ref,
    inputs, cot, field, seen, gates, dfield, ahead,
):
    segment = white_ref.shape[1]
    layer_count = mix_ref.shape[0]
    channels = mix_ref.shape[1]
    lane = lax.broadcasted_iota(jnp.int32, (channels, TILE), 1)

    def at(column):
        return MARGIN + column

    bins = bins_ref[...]
    table_rows = psd_ref.shape[0] // 2
    row_at = lax.broadcasted_iota(jnp.int32, bins.shape, 0)
    first_row = jnp.where(lax.rem(row_at, 4) < 2, 0, table_rows)
    entry_row = lax.shift_right_logical(bins, 7) + first_row
    entry_lane = jnp.bitwise_and(bins, TILE - 1)
    factor = jnp.zeros(bins.shape, F32)
    for row in range(2 * table_rows):
        table = jnp.broadcast_to(psd_ref[row : row + 1, :], (bins.shape[0], TILE))
        found = jnp.take_along_axis(table, entry_lane, axis=1)
        factor = jnp.where(entry_row == row, found, factor)
    factor_ref[...] = factor

    inputs[:, 0:MARGIN] = left_ref[...]
    inputs[:, MARGIN : MARGIN + segment] = white_ref[...]
    inputs[:, MARGIN + segment :] = right_ref[...]
    cot[:, 0:segment] = cot_ref[...]
    cot[:, segment:] = cot_right_ref[...]

    lift = lift_ref[...]
    field[0, :, 0:FRONT] = jnp.zeros((channels, FRONT), F32)
    field[1, :, 0:FRONT] = jnp.zeros((channels, FRONT), F32)
    for start, stop in chunks_of(-MARGIN, segment + MARGIN):
        x = inputs[:, at(start) : at(stop)]
        field[0, :, FRONT + at(start) : FRONT + at(stop)] = (
            lift[:, 0:1] * x[0:1] + lift[:, 1:2] * x[1:2] + lift[:, 2:3] * x[2:3]
        )

    for layer in range(layer_count):
        delay = dil_ref[layer]
        tiles_back = delay // TILE
        rest = delay - tiles_back * TILE
        weight = jnp.concatenate([now_ref[layer], past_ref[layer]], axis=1)
        mix = mix_ref[layer]
        source, target = layer % 2, (layer + 1) % 2
        first = -DMAX * (layer_count - 1 - layer)
        for start, stop in chunks_of(first, segment + MARGIN):
            size = stop - start
            place = FRONT + at(start)
            now = field[source, :, place : place + size]
            begin = pl.multiple_of(place - TILE - tiles_back * TILE, TILE)
            window = field[source, :, pl.ds(begin, size + TILE)]
            turned = [
                pltpu.roll(window[:, TILE * i : TILE * (i + 1)], rest, 1)
                for i in range(size // TILE + 1)
            ]
            past = jnp.concatenate(
                [
                    jnp.where(lane < rest, turned[i], turned[i + 1])
                    for i in range(size // TILE)
                ],
                axis=1,
            )
            both = jnp.concatenate([now, past], axis=0).astype(BF16)
            pre = jnp.dot(weight, both, preferred_element_type=F32)
            filt = jnp.tanh(pre[:channels])
            sig = 0.5 * jnp.tanh(0.5 * pre[channels:]) + 0.5
            gate = (filt * sig).astype(BF16)
            if layer + 1 < layer_count:
                field[target, :, place : place + size] = now + jnp.dot(
                    mix, gate, preferred_element_type=F32
                )
            if start >= 0:
                seen[layer, 0 : 2 * channels, start:stop] = both
                seen[layer, 2 * channels :, start:stop] = gate
                gates[layer, 0:channels, start:stop] = filt
                gates[layer, channels:, start:stop] = sig

    mixes = []
    ahead[...] = jnp.zeros(ahead.shape, F32)
    for layer in reversed(range(layer_count)):
        delay = dil_ref[layer]
        tiles_on = delay // TILE
        rest = delay - tiles_on * TILE
        back = jnp.where(rest == 0, 0, TILE - rest)
        weight_t = jnp.concatenate([now_ref[layer], past_ref[layer]], axis=1).T
        mix_t = mix_ref[layer].T
        reach = min(MARGIN, DMAX * (layer + 1))
        total = jnp.zeros((3 * channels, 3 * channels), F32)
        for start, stop in reversed(chunks_of(0, segment + reach)):
            size = stop - start
            if layer == layer_count - 1:
                grad_b = cot[:, start:stop]
                grad = grad_b.astype(F32)
            else:
                grad = dfield[:, start:stop]
                grad_b = grad.astype(BF16)
            filt = gates[layer, 0:channels, start:stop]
            sig = gates[layer, channels:, start:stop]
            dgate = jnp.dot(mix_t, grad_b, preferred_element_type=F32)
            dgate_sig = dgate * sig
            dpre = jnp.concatenate(
                [dgate_sig * (1.0 - filt * filt), dgate_sig * filt * (1.0 - sig)], axis=0
            ).astype(BF16)
            terms = jnp.dot(weight_t, dpre, preferred_element_type=F32)
            ahead[:, start:stop] = terms[channels:]
            begin = pl.multiple_of(start + tiles_on * TILE, TILE)
            window = ahead[:, pl.ds(begin, size + TILE)]
            turned = [
                pltpu.roll(window[:, TILE * i : TILE * (i + 1)], back, 1)
                for i in range(size // TILE + 1)
            ]
            moved = jnp.concatenate(
                [
                    jnp.where(lane < TILE - rest, turned[i], turned[i + 1])
                    for i in range(size // TILE)
                ],
                axis=1,
            )
            dfield[:, start:stop] = grad + terms[:channels] + moved
            if start < segment:
                left = jnp.concatenate([dpre, grad_b], axis=0)
                total += lax.dot_general(
                    left, seen[layer, :, start:stop], (((1,), (1,)), ((), ())),
                    preferred_element_type=F32,
                )
        grads_ref[2 * channels * layer : 2 * channels * (layer + 1), :] = total[
            : 2 * channels, : 2 * channels
        ].astype(BF16)
        mixes.append(total[2 * channels :, 2 * channels :])

    lift_total = jnp.zeros((channels, 3), F32)
    lift_t = lift.T
    for start, stop in chunks_of(0, segment):
        grad = dfield[:, start:stop]
        x = inputs[:, at(start) : at(stop)]
        part = jnp.dot(lift_t, grad, preferred_element_type=F32, precision=lax.Precision.HIGHEST)
        part = jnp.concatenate([part, jnp.zeros((1, stop - start), F32)], axis=0)
        if dinput_ref.ndim == 3:
            for i in range((stop - start) // TILE):
                dinput_ref[start // TILE + i] = part[:, TILE * i : TILE * (i + 1)]
        else:
            dinput_ref[:, start:stop] = part
        lift_total += lax.dot_general(
            grad, x, (((1,), (1,)), ((), ())), preferred_element_type=F32,
            precision=lax.Precision.HIGHEST,
        )
    last = 2 * channels * layer_count
    grads_ref[last : last + channels, :] = jnp.concatenate([mixes[2], mixes[1]], axis=1).astype(BF16)
    grads_ref[last + channels :, :] = jnp.concatenate(
        [mixes[0], lift_total, jnp.zeros((channels, channels - 3), F32)], axis=1
    ).astype(BF16)


def filter_kernel(
    rows_count, cols_count,
    x_ref, grads_ref, factor_ref, turn_a_ref, turn_b_ref, spread_ref, local_ref, fast_ref,
    fast_back_ref, local_back_ref, gather_ref, twiddle_ref,
    out_ref, sums_ref,
    got_x, spectra, got_spectra, parts, got_parts, result, got_result, got_grads, own_sum, all_sums,
    send_sems, recv_sems,
):
    groups = rows_count * cols_count
    small = x_ref.shape[2]
    me = lax.axis_index("rows") * cols_count + lax.axis_index("cols")

    def peer_of(step):
        peer = lax.rem(me + step, groups)
        return peer, (peer // cols_count, lax.rem(peer, cols_count))

    barrier = pltpu.get_barrier_semaphore()

    def greet(step, carry):
        _, device = peer_of(step)
        pl.semaphore_signal(barrier, inc=1, device_id=device, device_id_type=pl.DeviceIdType.MESH)
        return carry

    lax.fori_loop(1, groups, greet, 0)
    pl.semaphore_wait(barrier, groups - 1)

    def exchange(slot, source, target, whole=False):
        def send(step, carry):
            peer, device = peer_of(step)
            pltpu.make_async_remote_copy(
                src_ref=source if whole else source.at[peer],
                dst_ref=target.at[me],
                send_sem=send_sems.at[slot],
                recv_sem=recv_sems.at[slot],
                device_id=device,
                device_id_type=pl.DeviceIdType.MESH,
            ).start()
            return carry

        lax.fori_loop(1, groups, send, 0)
        target[me] = source[...] if whole else source[me]

    def wait_for(sems, slot, target):
        some = target.at[pl.ds(0, groups - 1)]
        pltpu.make_async_copy(some, some, sems.at[slot]).wait()

    flat = (4 * groups, small)
    cube = (groups, 4, small)
    exchange(0, x_ref, got_x)
    exchange(1, grads_ref, got_grads)

    wait_for(recv_sems, 0, got_x)
    both = dot_left(spread_ref, got_x[...].reshape(flat))
    spectra[...] = (
        both[: 4 * groups] * turn_a_ref[0] + both[4 * groups :] * turn_a_ref[1]
    ).reshape(cube)
    exchange(2, spectra, got_spectra)

    wait_for(recv_sems, 1, got_grads)
    total = got_grads[0].astype(F32)
    for i in range(1, groups):
        total += got_grads[i].astype(F32)
    own_sum[...] = total.astype(BF16)
    exchange(3, own_sum, all_sums, whole=True)

    wait_for(recv_sems, 2, got_spectra)
    both = dot_left(local_ref, got_spectra[...].reshape(flat))
    here, turned = both[: 4 * groups], both[4 * groups :]
    cosine, sine = twiddle_ref[0], twiddle_ref[1]
    pair = jnp.concatenate([here * cosine - turned * sine, turned * cosine + here * sine], axis=1)
    pair = dot_right(pair, fast_ref)
    factor = factor_ref[...]
    pair = jnp.concatenate([pair[:, :small] * factor, pair[:, small:] * factor], axis=1)
    pair = dot_right(pair, fast_back_ref)
    here, turned = pair[:, :small], pair[:, small:]
    pair = jnp.concatenate([here * cosine + turned * sine, turned * cosine - here * sine], axis=1)
    pair = dot_left(local_back_ref, pair)
    parts[...] = (pair[:, :small] * turn_b_ref[0] + pair[:, small:] * turn_b_ref[1]).reshape(cube)
    exchange(4, parts, got_parts)

    wait_for(recv_sems, 4, got_parts)
    result[...] = dot_left(gather_ref, got_parts[...].reshape(flat)).reshape(cube)
    exchange(5, result, got_result)

    wait_for(recv_sems, 3, all_sums)
    sums_ref[...] = all_sums[...]
    wait_for(recv_sems, 5, got_result)
    if out_ref.ndim == 2:
        for i in range(groups):
            out_ref[:, small * i : small * (i + 1)] = got_result[i][:3]
    else:
        out_ref[...] = got_result[...]
    for slot, target in enumerate(
        (got_x, got_grads, got_spectra, all_sums, got_parts, got_result)
    ):
        wait_for(send_sems, slot, target)


def constants(rows_count, cols_count, small):
    groups = rows_count * cols_count
    segment = groups * small
    ids = np.arange(groups)
    residues = ids // cols_count + rows_count * (ids % cols_count)
    unit = np.eye(4)
    swap = np.kron(np.eye(2), np.array([[0.0, -1.0], [1.0, 0.0]]))
    take = np.diag([1.0, 1.0, 1.0, 0.0])

    def blocks(left, right, sign, inner):
        angle = sign * 2.0 * np.pi / groups * (np.outer(left, right) % groups)
        return np.kron(np.cos(angle), unit @ inner) + np.kron(np.sin(angle), swap @ inner)

    turn_all = np.kron(np.eye(groups), swap)
    spread = blocks(residues, ids, -1.0, take)
    local = blocks(ids, ids, -1.0, unit)
    local_back = blocks(ids, ids, 1.0, unit)
    gather = np.kron(np.eye(groups), take) @ blocks(ids, residues, 1.0, unit)
    gather = gather / float(segment * groups)
    lanes = np.arange(small)
    angle = 2.0 * np.pi / small * (np.outer(lanes, lanes) % small)
    cosine, sine = np.cos(angle), np.sin(angle)
    fast = np.block([[cosine, sine], [-sine, cosine]])
    fast_back = np.block([[cosine, -sine], [sine, cosine]])
    angle = 2.0 * np.pi / segment * (np.outer(ids, lanes) % segment)
    angle = np.repeat(angle, 4, axis=0)
    twiddle = np.stack([np.cos(angle), np.sin(angle)]).astype(np.float32)
    return (
        residues,
        halves(np.concatenate([spread, turn_all @ spread])),
        halves(np.concatenate([local, turn_all @ local])),
        halves(fast),
        halves(fast_back),
        halves(local_back),
        halves(gather),
        twiddle,
    )


def turns(angle_steps, length, sign):
    angle = sign * 2.0 * math.pi / length * (angle_steps % length).astype(F32)
    angle = jnp.repeat(angle, 4, axis=0)
    return jnp.stack([jnp.cos(angle), jnp.sin(angle)])


def vmem():
    return pl.BlockSpec(memory_space=pltpu.VMEM)


def solution(mesh):
    rows_count, cols_count = mesh.shape["rows"], mesh.shape["cols"]
    groups = rows_count * cols_count

    def local(whitened, cotangent, lift, now, past, mix, dilations, psd_bin, psd_weight):
        segment = whitened.shape[1]
        layer_count, channels = mix.shape[:2]
        small = segment // groups
        length = segment * groups
        me = lax.axis_index("rows") * cols_count + lax.axis_index("cols")
        residue = lax.axis_index("rows") + rows_count * lax.axis_index("cols")
        onward = [(i, i + 1) for i in range(groups - 1)]
        backward = [(i + 1, i) for i in range(groups - 1)]
        both_axes = ("rows", "cols")
        cot_right = lax.ppermute(cotangent[:, :MARGIN], both_axes, backward)
        left = lax.ppermute(whitened[:, segment - MARGIN :], both_axes, onward)
        right = lax.ppermute(whitened[:, :MARGIN], both_axes, backward)

        residues, spread, local_m, fast, fast_back, local_back, gather, twiddle = constants(
            rows_count, cols_count, small
        )
        samples = jnp.arange(small, dtype=jnp.int32)
        group_ids = jnp.arange(groups, dtype=jnp.int32)
        turn_a = turns(
            jnp.asarray(residues, jnp.int32)[:, None] * (me * small + samples)[None, :], length, -1.0
        )
        turn_b = turns(residue * (group_ids[:, None] * small + samples[None, :]), length, 1.0)

        wide = small == TILE
        bins = jnp.repeat(psd_bin.reshape(small, groups).T, 4, axis=0).reshape(-1, TILE)
        if not wide:
            bins = jnp.tile(psd_bin.reshape(small, groups).T.reshape(-1, 1, TILE), (1, 4, 1))
            bins = bins.reshape(-1, TILE)
        dinput_shape = (groups, 4, small) if wide else (4, segment)
        grad_rows = 2 * channels * (layer_count + 1)
        reach = segment + MARGIN
        dinput, grads, factor = pl.pallas_call(
            layers_kernel,
            out_shape=(
                jax.ShapeDtypeStruct(dinput_shape, F32),
                jax.ShapeDtypeStruct((grad_rows, 2 * channels), BF16),
                jax.ShapeDtypeStruct(bins.shape, F32),
            ),
            in_specs=[pl.BlockSpec(memory_space=pltpu.SMEM)] + [vmem()] * 11,
            out_specs=(vmem(),) * 3,
            scratch_shapes=[
                pltpu.VMEM((3, reach + MARGIN), F32),
                pltpu.VMEM((channels, reach), BF16),
                pltpu.VMEM((2, channels, FRONT + MARGIN + reach), F32),
                pltpu.VMEM((layer_count, 3 * channels, reach), BF16),
                pltpu.VMEM((layer_count, 2 * channels, reach), F32),
                pltpu.VMEM((channels, reach), F32),
                pltpu.VMEM((channels, reach + 3 * TILE), F32),
            ],
            compiler_params=pltpu.CompilerParams(vmem_limit_bytes=48 * 2**20),
            name="layers",
        )(
            dilations, whitened, left, right, cotangent, cot_right, lift, now, past, mix, bins,
            psd_weight.reshape(-1, TILE),
        )
        if not wide:
            dinput = dinput.reshape(4, groups, small).transpose(1, 0, 2)
            factor = factor.reshape(-1, 4, TILE).transpose(1, 0, 2).reshape(4, groups, small)
            factor = factor.transpose(1, 0, 2).reshape(4 * groups, small)
        cube = (groups, 4, small)
        share = (groups, grad_rows // groups, 2 * channels)
        out, sums = pl.pallas_call(
            lambda *refs: filter_kernel(rows_count, cols_count, *refs),
            out_shape=(
                jax.ShapeDtypeStruct((3, segment) if wide else cube, F32),
                jax.ShapeDtypeStruct(share, BF16),
            ),
            in_specs=[vmem()] * 12,
            out_specs=(vmem(),) * 2,
            scratch_shapes=[pltpu.VMEM(cube, F32)] * 7
            + [
                pltpu.VMEM(share, BF16),
                pltpu.VMEM(share[1:], BF16),
                pltpu.VMEM(share, BF16),
                pltpu.SemaphoreType.DMA((6,)),
                pltpu.SemaphoreType.DMA((6,)),
            ],
            compiler_params=pltpu.CompilerParams(
                collective_id=0, has_side_effects=True, vmem_limit_bytes=56 * 2**20
            ),
            name="whiten",
        )(
            dinput, grads.reshape(share), factor, turn_a, turn_b, spread, local_m, fast, fast_back,
            local_back, gather, twiddle,
        )
        if not wide:
            out = out.transpose(1, 0, 2).reshape(4, segment)[:3]
        scaling = 1.0 / math.sqrt(float(length))
        sums = sums.reshape(grad_rows, 2 * channels).astype(F32) * scaling
        last = 2 * channels * layer_count
        taps = sums[:last].reshape(layer_count, 2 * channels, 2 * channels)
        pair = sums[last : last + channels]
        rest = sums[last + channels :]
        mixes = jnp.stack([pair[:, :channels], pair[:, channels:], rest[:, :channels]])
        return (
            out,
            taps[:, :, :channels],
            taps[:, :, channels:],
            mixes,
            rest[:, channels : channels + 3],
        )

    in_specs = (
        P(None, ("rows", "cols")),
        P(None, ("rows", "cols")),
        P(),
        P(),
        P(),
        P(),
        P(),
        P(None, "cols", "rows"),
        P(),
    )
    out_specs = (P(None, ("rows", "cols")), P(), P(), P(), P())
    return jax.shard_map(local, mesh=mesh, in_specs=in_specs, out_specs=out_specs, check_vma=False)
```

profile of v0, /device:TPU:0, one launch (start us, length us, event | category | flops | bytes accessed | tf_op | source)
XLA Modules:
  0.0 65.9 jit_solution(4295351296193732447)
XLA Ops:
  0.6 0.7 %fusion.11 = (f32[3,640]{1,0:T(4,128)S(1)}, f32[3,640]{1,0:T(4,128)S(1)}) fusion(f32[3,4096]{1,0:T(4,128)} %white_ref.1), kind=kLoop, calls=%fused_computation.28 | loop fusion | bytes 30720 | tf_op jit(solution)/shard_map/slice | solution.py:370
  1.4 2.3 %collective-permute-start = (f32[3,640]{1,0:T(4,128)S(1)}, f32[3,640]{1,0:T(4,128)S(1)}, u32[]{:S(2)}, u32[]{:S(2)}) collective-permute-start(f32[3,640]{1,0:T(4,128)S(1)} %get-tuple-element.21), channel_id=1, source_target_pairs={{0,1},{1,2},{2,3},{3,4},{4,5},{5,6},{6,7},{7,8},{8,9},{9,10},{10,1... | collective-permute-start | bytes 23048 | tf_op jit(solution)/shard_map/ppermute | solution.py:369
  3.7 1.3 %collective-permute-start.1 = (f32[3,640]{1,0:T(4,128)S(1)}, f32[3,640]{1,0:T(4,128)S(1)}, u32[]{:S(2)}, u32[]{:S(2)}) collective-permute-start(f32[3,640]{1,0:T(4,128)S(1)} %get-tuple-element.20), channel_id=1, source_target_pairs={{1,0},{2,1},{3,2},{4,3},{5,4},{6,5},{7,6},{8,7},{9,8},{10,9},{11,1... | collective-permute-start | bytes 23048 | tf_op jit(solution)/shard_map/ppermute | solution.py:370
  5.0 0.9 %slice.39 = bf16[64,640]{1,0:T(8,128)(2,1)S(1)} slice(bf16[64,4096]{1,0:T(8,128)(2,1)} %cot_ref.1), slice={[0:64], [0:640]} | slice | bytes 163840 | tf_op jit(solution)/shard_map/slice | solution.py:368
  5.9 1.3 %collective-permute-start.2 = (bf16[64,640]{1,0:T(8,128)(2,1)S(1)}, bf16[64,640]{1,0:T(8,128)(2,1)S(1)}, u32[]{:S(2)}, u32[]{:S(2)}) collective-permute-start(bf16[64,640]{1,0:T(8,128)(2,1)S(1)} %slice.39), channel_id=1, source_target_pairs={{1,0},{2,1},{3,2},{4,3},{5,4},{6,5},{7,6},{8,7},{9,8},{10,9},{11,1... | collective-permute-start | bytes 245768 | tf_op jit(solution)/shard_map/ppermute | solution.py:368
  7.2 0.6 copy-done.13
  7.9 0.1 fusion.9
  8.0 0.2 fusion.7
  8.3 0.7 %pad_maximum_fusion = (f32[2,128,128]{2,1,0:T(8,128)}, f32[2,128,128]{2,1,0:T(8,128)}) fusion(f32[1,128,128]{2,1,0:T(8,128)S(1)} %bitcast.22, f32[1,128,128]{2,1,0:T(8,128)S(1)} %bitcast.23, f32[1,128,128]{2,1,0:T(8,128)S(1)} %bitcast.24, f32[1,128,128]{2,1,0:T(8,128)S(1)} %bitcast.25), kind=kLoop, calls=%fused_computation.1 | loop fusion | flops 65536 | bytes 524288 | tf_op jit(solution)/shard_map/stack | solution.py:347
  9.1 0.1 copy.30.lift_ref
  9.2 0.1 copy.31.now_ref
  9.3 0.7 %copy-done.9 = bf16[3,128,64]{1,2,0:T(8,128)(2,1)S(1)} copy-done((bf16[3,128,64]{1,2,0:T(8,128)(2,1)S(1)}, bf16[3,128,64]{1,2,0:T(8,128)(2,1)}, u32[]{:S(2)}) %copy-start.9) | copy-done | bytes 49176
  10.0 0.1 copy.32.past_ref
  10.1 0.5 broadcast.36
  10.7 0.7 %reduce.3 = s32[4096]{0:T(1024)S(1)} reduce(s32[4096,1,1]{0,2,1:T(1,128)S(1)} %copy-done.10, s32[]{:T(128)} %broadcast.36), dimensions={1,2}, to_apply=%param.24.reduce_sub_computation.3 | reduce | bytes 32772 | tf_op args[7]
  11.4 0.1 reshape.87
  11.5 0.6 copy-done.11
  12.3 0.7 %copy-done.2 = f32[3,4096]{1,0:T(4,128)S(1)} copy-done((f32[3,4096]{1,0:T(4,128)S(1)}, f32[3,4096]{1,0:T(4,128)}, u32[]{:S(2)}) %copy-start.2) | copy-done | bytes 49176
  13.0 14.0 %layers.1 = (f32[32,4,128]{2,1,0:T(4,128)S(1)}, bf16[512,128]{1,0:T(8,128)(2,1)S(1)}, f32[128,128]{1,0:T(8,128)S(1)}) custom-call(s32[3]{0:T(128)S(1)} %copy-done.6, f32[3,4096]{1,0:T(4,128)S(1)} %copy-done.2, f32[3,640]{1,0:T(4,128)S(1)} %collective-permute-done.left_ref, f32[3,640]{1,0:T(4,128)S(1)} %collective-permute-done.1.right_ref, ...), custom_call_target="tpu_custom_call" | custom-call | tf_op jit(solution)/shard_map/layers/pallas_call | solution.py:390
  27.0 0.6 copy-done.1
  27.6 0.6 copy-done.3
  28.2 0.6 copy-done.4
  28.9 32.2 %whiten.1 = (f32[3,4096]{1,0:T(4,128)}, bf16[32,16,128]{2,1,0:T(8,128)(2,1)}) custom-call(f32[32,4,128]{2,1,0:T(4,128)} %copy-done.3, bf16[32,16,128]{2,1,0:T(8,128)(2,1)} %bitcast.17, f32[128,128]{1,0:T(8,128)} %copy-done.4, f32[2,128,128]{2,1,0:T(8,128)} %get-tuple-element.26.refs_3_, f32[2,128,128]{2,1,0:T(8,128)} %get-tuple-element.27.refs_4_, ...), custom_call_target="tpu_custom_call" | custom-call | tf_op jit(solution)/shard_map/whiten/pallas_call | solution.py:420
  61.1 0.9 %convert_multiply_fusion = f32[32,16,128]{2,1,0:T(8,128)S(1)} fusion(bf16[32,16,128]{2,1,0:T(8,128)(2,1)} %get-tuple-element.14), kind=kLoop, calls=%fused_computation | loop fusion | flops 131072 | bytes 393216 | tf_op jit(solution)/shard_map/mul | solution.py:447
  62.0 0.1 slice_bitcast_fusion.2
  62.2 0.1 fusion.10
  62.3 0.8 %copy.36 = f32[3,128,64]{1,2,0:T(8,128)} copy(f32[3,128,64]{2,1,0:T(8,128)S(1)} %get-tuple-element.19) | data formatting | bytes 196608
  63.1 0.8 %copy.37 = f32[3,128,64]{1,2,0:T(8,128)} copy(f32[3,128,64]{2,1,0:T(8,128)S(1)} %get-tuple-element.18) | data formatting | bytes 196608
  63.8 0.7 copy.38
  64.5 0.6 pad_maximum_fusion.2
  65.1 0.2 copy-done.7
  65.3 0.6 copy.40
  (34 shorter events, 0.4 us)
Async XLA Ops:
  1.4 10.8 %collective-permute-start = (f32[3,640]{1,0:T(4,128)S(1)}, f32[3,640]{1,0:T(4,128)S(1)}, u32[]{:S(2)}, u32[]{:S(2)}) collective-permute-start(f32[3,640]{1,0:T(4,128)S(1)} %get-tuple-element.21), channel_id=1, source_target_pairs={{0,1},{1,2},{2,3},{3,4},{4,5},{5,6},{6,7},{7,8},{8,9},{9,10},{10,1... | collective-permute-start | bytes 23048 | tf_op jit(solution)/shard_map/ppermute | solution.py:369
  3.7 8.5 %collective-permute-start.1 = (f32[3,640]{1,0:T(4,128)S(1)}, f32[3,640]{1,0:T(4,128)S(1)}, u32[]{:S(2)}, u32[]{:S(2)}) collective-permute-start(f32[3,640]{1,0:T(4,128)S(1)} %get-tuple-element.20), channel_id=1, source_target_pairs={{1,0},{2,1},{3,2},{4,3},{5,4},{6,5},{7,6},{8,7},{9,8},{10,9},{11,1... | collective-permute-start | bytes 23048 | tf_op jit(solution)/shard_map/ppermute | solution.py:370
  5.9 6.3 %collective-permute-start.2 = (bf16[64,640]{1,0:T(8,128)(2,1)S(1)}, bf16[64,640]{1,0:T(8,128)(2,1)S(1)}, u32[]{:S(2)}, u32[]{:S(2)}) collective-permute-start(bf16[64,640]{1,0:T(8,128)(2,1)S(1)} %slice.39), channel_id=1, source_target_pairs={{1,0},{2,1},{3,2},{4,3},{5,4},{6,5},{7,6},{8,7},{9,8},{10,9},{11,1... | collective-permute-start | bytes 245768 | tf_op jit(solution)/shard_map/ppermute | solution.py:368
  7.2 0.7 copy-start.13
  8.3 0.8 %copy-start.12 = (f32[64,3]{0,1:T(4,128)S(1)}, f32[64,3]{0,1:T(4,128)}, u32[]{:S(2)}) copy-start(f32[64,3]{0,1:T(4,128)} %param.19) | copy-start | bytes 2308
  8.3 0.9 %copy-start.8 = (bf16[3,128,64]{1,2,0:T(8,128)(2,1)S(1)}, bf16[3,128,64]{1,2,0:T(8,128)(2,1)}, u32[]{:S(2)}) copy-start(bf16[3,128,64]{1,2,0:T(8,128)(2,1)} %param.20) | copy-start | bytes 147460
  8.3 3.9 %copy-start = (bf16[64,4096]{1,0:T(8,128)(2,1)S(1)}, bf16[64,4096]{1,0:T(8,128)(2,1)}, u32[]{:S(2)}) copy-start(bf16[64,4096]{1,0:T(8,128)(2,1)} %cot_ref.1) | copy-start | bytes 1572868
  9.2 0.8 %copy-start.9 = (bf16[3,128,64]{1,2,0:T(8,128)(2,1)S(1)}, bf16[3,128,64]{1,2,0:T(8,128)(2,1)}, u32[]{:S(2)}) copy-start(bf16[3,128,64]{1,2,0:T(8,128)(2,1)} %param.21) | copy-start | bytes 147460
  10.0 0.7 %copy-start.10 = (s32[4096,1,1]{0,2,1:T(1,128)S(1)}, s32[4096,1,1]{0,2,1:T(1,128)}, u32[]{:S(2)}) copy-start(s32[4096,1,1]{0,2,1:T(1,128)} %param.24) | copy-start | bytes 49156
  11.4 0.7 %copy-start.11 = (f32[2,1024]{1,0:T(2,128)S(1)}, f32[2,1024]{1,0:T(2,128)}, u32[]{:S(2)}) copy-start(f32[2,1024]{1,0:T(2,128)} %param.25) | copy-start | bytes 24580
  11.4 0.8 %copy-start.5 = (bf16[3,64,64]{2,1,0:T(8,128)(2,1)S(1)}, bf16[3,64,64]{2,1,0:T(8,128)(2,1)}, u32[]{:S(2)}) copy-start(bf16[3,64,64]{2,1,0:T(8,128)(2,1)} %mix_ref.1) | copy-start | bytes 73732
  12.1 0.8 %copy-start.2 = (f32[3,4096]{1,0:T(4,128)S(1)}, f32[3,4096]{1,0:T(4,128)}, u32[]{:S(2)}) copy-start(f32[3,4096]{1,0:T(4,128)} %white_ref.1) | copy-start | bytes 147460
  12.2 0.8 %copy-start.6 = (s32[3]{0:T(128)S(1)}, s32[3]{0:T(128)}, u32[]{:S(2)}) copy-start(s32[3]{0:T(128)} %dil_ref.1) | copy-start | bytes 40
  27.0 0.7 copy-start.1
  27.6 0.6 copy-start.3
  28.2 0.6 copy-start.4
  64.5 0.8 %copy-start.7 = (f32[3,4096]{1,0:T(4,128)S(1)}, f32[3,4096]{1,0:T(4,128)}, u32[]{:S(2)}) copy-start(f32[3,4096]{1,0:T(4,128)} %get-tuple-element.33) | copy-start | bytes 147460
where the time goes:
time: 66.5 us; the launch traced here: 65.9 us
  Pallas kernels  46.2 us (69%)
  local copies, waits for them, and re-layouts  10.7 us (16%)
  starting transfers between devices  4.92 us (7%)
  other arithmetic  3.3 us (5%)
  between operations  0.89 us (1%)
    pallas_call x1, Pallas kernels, local(): pl.pallas_call(lambda *refs: filter_kernel(rows_count, cols_count, *refs)...  32.2 us
    pallas_call x1, Pallas kernels, local(): pl.pallas_call(layers_kernel, out_shape=(jax.ShapeDtypeStruct(dinput_shap...  14 us
    unnamed x36, local copies, waits for them, and re-layouts  8.56 us
    ppermute x1, starting transfers between devices, local(): left = lax.ppermute(whitened[:, segment - MARGIN:], both_axes, onward)  2.35 us
  transfers between devices with their start and end apart: 3, of which 0 were waited for; matrix products, arithmetic and copies ran while one was open for 6% of the time, Pallas kernels for 0%

commit v1 on v0

v1 whole, which is shorter than its diff:
```python
import math

import jax
import jax.numpy as jnp
import numpy as np
from jax import lax
from jax.experimental import pallas as pl
from jax.experimental.pallas import tpu as pltpu
from jax.sharding import PartitionSpec as P

DMAX = 256
TILE = 128
WIDE = 256
MARGIN = 640
FRONT = 384
F32 = jnp.float32
BF16 = jnp.bfloat16


def halves(matrix):
    high = matrix.astype(np.float32).astype(jnp.bfloat16)
    low = (matrix - high.astype(np.float64)).astype(np.float32).astype(jnp.bfloat16)
    return np.stack([high, low])


def split(values):
    high = values.astype(BF16)
    return high, (values - high.astype(F32)).astype(BF16)


def dot_left(pair_ref, values):
    high, low = split(values)
    total = jnp.dot(pair_ref[0], high, preferred_element_type=F32)
    total += jnp.dot(pair_ref[0], low, preferred_element_type=F32)
    return total + jnp.dot(pair_ref[1], high, preferred_element_type=F32)


def dot_right(values, pair_ref):
    high, low = split(values)
    total = jnp.dot(high, pair_ref[0], preferred_element_type=F32)
    total += jnp.dot(low, pair_ref[0], preferred_element_type=F32)
    return total + jnp.dot(high, pair_ref[1], preferred_element_type=F32)


def chunks_of(first, last, size=1024):
    cuts = sorted({first, last} | {x for x in range(0, last, size) if first < x < last})
    return list(zip(cuts[:-1], cuts[1:]))


def factors_kernel(bins_ref, psd_ref, factor_ref):
    bins = bins_ref[...]
    table_rows = psd_ref.shape[0] // 2
    row_at = lax.broadcasted_iota(jnp.int32, bins.shape, 0)
    first_row = jnp.where(lax.rem(row_at, 4) < 2, 0, table_rows)
    entry_row = lax.shift_right_logical(bins, 7) + first_row
    entry_lane = jnp.bitwise_and(bins, TILE - 1)
    factor = jnp.zeros(bins.shape, F32)
    for row in range(2 * table_rows):
        table = jnp.broadcast_to(psd_ref[row : row + 1, :], (bins.shape[0], TILE))
        found = jnp.take_along_axis(table, entry_lane, axis=1)
        factor = jnp.where(entry_row == row, found, factor)
    factor_ref[...] = factor


def layers(
    before_halos, halos,
    dil_ref, white_ref, cot_ref, lift_ref, now_ref, past_ref, mix_ref,
    dinput_ref, grads_ref, inputs, cot, field, seen, gates, dfield, ahead,
):
    segment = white_ref.shape[1]
    layer_count = mix_ref.shape[0]
    channels = mix_ref.shape[1]
    offset = lax.broadcasted_iota(jnp.int32, (DMAX + WIDE, WIDE), 0)
    offset -= lax.broadcasted_iota(jnp.int32, (DMAX + WIDE, WIDE), 1)

    def picks(distance):
        return jnp.where(offset == distance, 1.0, 0.0).astype(BF16)

    def moved(window, matrix):
        size = window.shape[1] - DMAX
        rows = window.shape[0]
        full = size // WIDE * WIDE
        pieces = []
        if full:
            stacked = jnp.concatenate(
                [window[:, i : i + DMAX + WIDE] for i in range(0, full, WIDE)], axis=0
            )
            found = jnp.dot(stacked, matrix, preferred_element_type=F32).astype(BF16)
            pieces = [found[rows * i : rows * (i + 1)] for i in range(full // WIDE)]
        if full < size:
            part = matrix[: DMAX + size - full, : size - full]
            found = jnp.dot(window[:, full:], part, preferred_element_type=F32)
            pieces.append(found.astype(BF16))
        return jnp.concatenate(pieces, axis=1)

    def at(column):
        return MARGIN + column

    inputs[:, MARGIN : MARGIN + segment] = white_ref[...]
    cot[:, 0:segment] = cot_ref[...]
    lift_t = lift_ref[...]
    lift = lift_t.T
    field[0, :, 0:FRONT] = jnp.zeros((channels, FRONT), F32)
    field[1, :, 0:FRONT] = jnp.zeros((channels, FRONT), F32)
    def lifted(start, stop):
        x = inputs[:, at(start) : at(stop)]
        field[0, :, FRONT + at(start) : FRONT + at(stop)] = (
            lift[:, 0:1] * x[0:1] + lift[:, 1:2] * x[1:2] + lift[:, 2:3] * x[2:3]
        )

    def in_order(layer, first):
        chunks = chunks_of(first, segment + MARGIN)
        if layer > 0:
            yield from chunks
            return
        inner = [c for c in chunks if DMAX <= c[0] and c[1] <= segment]
        yield from inner
        left, right, cot_right = halos()
        inputs[:, 0:MARGIN] = left
        inputs[:, MARGIN + segment :] = right
        cot[:, segment:] = cot_right
        lifted(-MARGIN, 0)
        lifted(segment, segment + MARGIN)
        yield from [c for c in chunks if c not in inner]

    for start, stop in chunks_of(0, segment):
        lifted(start, stop)
    before_halos()

    for layer in range(layer_count):
        delays = dil_ref[layer : layer + 1, :]
        matrix = picks(DMAX - delays)
        weight = jnp.concatenate([now_ref[layer], past_ref[layer]], axis=0).T
        mix = mix_ref[layer]
        source, target = layer % 2, (layer + 1) % 2
        first = -DMAX * (layer_count - 1 - layer)
        for start, stop in in_order(layer, first):
            size = stop - start
            place = FRONT + at(start)
            now = field[source, :, place : place + size]
            past = moved(field[source, :, place - DMAX : place + size].astype(BF16), matrix)
            both = jnp.concatenate([now.astype(BF16), past], axis=0)
            pre = jnp.dot(weight, both, preferred_element_type=F32)
            filt = jnp.tanh(pre[:channels])
            sig = 0.5 * jnp.tanh(0.5 * pre[channels:]) + 0.5
            gate = (filt * sig).astype(BF16)
            if layer + 1 < layer_count:
                field[target, :, place : place + size] = now + jnp.dot(
                    mix, gate, preferred_element_type=F32
                )
            if start >= 0:
                seen[layer, 0 : 2 * channels, start:stop] = both
                seen[layer, 2 * channels :, start:stop] = gate
                gates[layer, 0:channels, start:stop] = filt
                gates[layer, channels:, start:stop] = sig

    taps, mixes = [], []
    ahead[...] = jnp.zeros(ahead.shape, BF16)
    for layer in reversed(range(layer_count)):
        delays = dil_ref[layer : layer + 1, :]
        matrix = picks(delays)
        weight_t = jnp.concatenate([now_ref[layer], past_ref[layer]], axis=1)
        mix_t = mix_ref[layer].T
        reach = min(MARGIN, DMAX * (layer + 1))
        total = jnp.zeros((3 * channels, 3 * channels), F32)
        for start, stop in reversed(chunks_of(0, segment + reach)):
            size = stop - start
            if layer == layer_count - 1:
                grad_b = cot[:, start:stop]
                grad = grad_b.astype(F32)
            else:
                grad = dfield[:, start:stop]
                grad_b = grad.astype(BF16)
            filt = gates[layer, 0:channels, start:stop]
            sig = gates[layer, channels:, start:stop]
            dgate = jnp.dot(mix_t, grad_b, preferred_element_type=F32)
            dgate_sig = dgate * sig
            dpre = jnp.concatenate(
                [dgate_sig * (1.0 - filt * filt), dgate_sig * filt * (1.0 - sig)], axis=0
            ).astype(BF16)
            ahead[:, start:stop] = dpre
            later = moved(ahead[:, start : stop + DMAX], matrix)
            dfield[:, start:stop] = grad + jnp.dot(
                weight_t, jnp.concatenate([dpre, later], axis=0), preferred_element_type=F32
            )
            if start < segment:
                left = jnp.concatenate([dpre, grad_b], axis=0)
                total += lax.dot_general(
                    seen[layer, :, start:stop], left, (((1,), (1,)), ((), ())),
                    preferred_element_type=F32,
                )
        taps.insert(0, total[: 2 * channels, : 2 * channels])
        mixes.insert(0, total[2 * channels :, 2 * channels :].T)

    lift_total = jnp.zeros((3, channels), F32)
    for start, stop in chunks_of(0, segment):
        grad = dfield[:, start:stop]
        x = inputs[:, at(start) : at(stop)]
        part = jnp.dot(lift_t, grad, preferred_element_type=F32, precision=lax.Precision.HIGHEST)
        part = jnp.concatenate([part, jnp.zeros((1, stop - start), F32)], axis=0)
        small = dinput_ref.shape[2]
        for i in range((stop - start) // small):
            dinput_ref[start // small + i] = part[:, small * i : small * (i + 1)]
        lift_total += lax.dot_general(
            x, grad, (((1,), (1,)), ((), ())), preferred_element_type=F32,
            precision=lax.Precision.HIGHEST,
        )
    lift_block = jnp.concatenate([lift_total, jnp.zeros((channels - 3, channels), F32)], axis=0)
    taps.append(
        jnp.concatenate(
            [
                jnp.concatenate([mixes[0], mixes[1]], axis=1),
                jnp.concatenate([mixes[2], lift_block], axis=1),
            ],
            axis=0,
        )
    )
    rows = jnp.concatenate(taps, axis=0)
    grads_ref[...] = rows.reshape(grads_ref.shape).astype(BF16)


def whole_kernel(
    rows_count, cols_count,
    dil_ref, white_ref, cot_ref, lift_ref, now_ref, past_ref, mix_ref, factor_ref,
    cos_a_ref, sin_a_ref, cos_b_ref, sin_b_ref, spread_ref, local_ref, fast_ref,
    fast_back_ref, local_back_ref, gather_ref, twiddle_ref,
    out_ref, sums_ref,
    inputs, cot, field, seen, gates, dfield, ahead, left_halo, right_halo, cot_halo, dinput, grads,
    got_x, spectra, got_spectra, parts, got_parts, result, got_result,
    got_cols, part_sums, got_rows, own_sum, sums_rows, sums_all,
    send_sems, recv_sems,
):
    groups = rows_count * cols_count
    segment = white_ref.shape[1]
    small = segment // groups
    my_row, my_col = lax.axis_index("rows"), lax.axis_index("cols")
    me = my_row * cols_count + my_col
    cols = [my_col] + [lax.rem(my_col + j, cols_count) for j in range(1, cols_count)]
    rows = [my_row] + [lax.rem(my_row + i, rows_count) for i in range(1, rows_count)]

    def for_others(body):
        for col in cols[1:]:
            body(my_row, col)

        def one_row(step, carry):
            row = lax.rem(my_row + step, rows_count)
            for col in cols:
                body(row, col)
            return carry

        lax.fori_loop(1, rows_count, one_row, 0)

    def send(slot, source, target, row, col):
        pltpu.make_async_remote_copy(
            src_ref=source,
            dst_ref=target,
            send_sem=send_sems.at[slot],
            recv_sem=recv_sems.at[slot],
            device_id=(row, col),
            device_id_type=pl.DeviceIdType.MESH,
        ).start()

    def wait_for(sems, slot, landed):
        pltpu.make_async_copy(landed, landed, sems.at[slot]).wait()

    def exchange(slot, source, target):
        def one(row, col):
            send(slot, source.at[row * cols_count + col], target.at[me], row, col)

        for_others(one)
        target[me] = source[me]

    barrier = pltpu.get_barrier_semaphore()

    def greet(row, col):
        pl.semaphore_signal(
            barrier, inc=1, device_id=(row, col), device_id_type=pl.DeviceIdType.MESH
        )

    for_others(greet)

    after = lax.rem(me + 1, groups)
    ahead_of = lax.rem(me + groups - 1, groups)
    halo_slots = ((6, left_halo), (7, right_halo), (8, cot_halo))

    def before_halos():
        pl.semaphore_wait(barrier, groups - 1)
        row, col = after // cols_count, lax.rem(after, cols_count)
        send(6, white_ref.at[:, pl.ds(segment - MARGIN, MARGIN)], left_halo, row, col)
        row, col = ahead_of // cols_count, lax.rem(ahead_of, cols_count)
        send(7, white_ref.at[:, pl.ds(0, MARGIN)], right_halo, row, col)
        send(8, cot_ref.at[:, pl.ds(0, MARGIN)], cot_halo, row, col)

    def halos():
        for slot, landed in halo_slots:
            wait_for(recv_sems, slot, landed)
        left = jnp.where(me == 0, 0.0, left_halo[...])
        right = jnp.where(me == groups - 1, 0.0, right_halo[...])
        cot_right = jnp.where(me == groups - 1, 0.0, cot_halo[...].astype(F32)).astype(BF16)
        return left, right, cot_right

    layers(
        before_halos, halos,
        dil_ref, white_ref, cot_ref, lift_ref, now_ref, past_ref, mix_ref,
        dinput, grads, inputs, cot, field, seen, gates, dfield, ahead,
    )

    flat = (4 * groups, small)
    cube = (groups, 4, small)

    def turned_by(values, cos_ref, sin_ref):
        here, turned = values
        cosine = jnp.broadcast_to(cos_ref[...][:, None, :], cube).reshape(flat)
        sine = jnp.broadcast_to(sin_ref[...][:, None, :], cube).reshape(flat)
        return (here * cosine + turned * sine).reshape(cube)

    exchange(0, dinput, got_x)
    for col in cols[1:]:
        send(1, grads.at[:, col], got_cols.at[my_col], my_row, col)
    got_cols[my_col] = grads[:, my_col]

    wait_for(recv_sems, 0, got_x.at[pl.ds(0, groups - 1)])
    both = dot_left(spread_ref, got_x[...].reshape(flat))
    spectra[...] = turned_by((both[: 4 * groups], both[4 * groups :]), cos_a_ref, sin_a_ref)
    exchange(2, spectra, got_spectra)

    wait_for(recv_sems, 1, got_cols.at[pl.ds(0, cols_count - 1)])
    total = got_cols[0].astype(F32)
    for i in range(1, cols_count):
        total += got_cols[i].astype(F32)
    part_sums[...] = total
    for row in rows[1:]:
        send(3, part_sums.at[row], got_rows.at[my_row], row, my_col)
    got_rows[my_row] = part_sums[my_row]

    wait_for(recv_sems, 2, got_spectra.at[pl.ds(0, groups - 1)])
    both = dot_left(local_ref, got_spectra[...].reshape(flat))
    here, turned = both[: 4 * groups], both[4 * groups :]
    cosine, sine = twiddle_ref[0], twiddle_ref[1]
    pair = jnp.concatenate([here * cosine - turned * sine, turned * cosine + here * sine], axis=1)
    pair = dot_right(pair, fast_ref)
    factor = factor_ref[...]
    pair = jnp.concatenate([pair[:, :small] * factor, pair[:, small:] * factor], axis=1)
    pair = dot_right(pair, fast_back_ref)
    here, turned = pair[:, :small], pair[:, small:]
    pair = jnp.concatenate([here * cosine + turned * sine, turned * cosine - here * sine], axis=1)
    pair = dot_left(local_back_ref, pair)
    parts[...] = turned_by((pair[:, :small], pair[:, small:]), cos_b_ref, sin_b_ref)
    exchange(4, parts, got_parts)

    wait_for(recv_sems, 3, got_rows.at[pl.ds(0, rows_count - 1)])
    total = got_rows[0]
    for i in range(1, rows_count):
        total += got_rows[i]
    own_sum[...] = total.astype(BF16)
    for row in rows[1:]:
        send(9, own_sum, sums_rows.at[my_row], row, my_col)
    sums_rows[my_row] = own_sum[...]

    wait_for(recv_sems, 4, got_parts.at[pl.ds(0, groups - 1)])
    result[...] = dot_left(gather_ref, got_parts[...].reshape(flat)).reshape(cube)
    exchange(5, result, got_result)

    wait_for(recv_sems, 9, sums_rows.at[pl.ds(0, rows_count - 1)])
    for col in cols[1:]:
        send(10, sums_rows, sums_all.at[:, my_col], my_row, col)
    sums_all[:, my_col] = sums_rows[...]

    wait_for(recv_sems, 5, got_result.at[pl.ds(0, groups - 1)])
    out_ref[...] = got_result[...]
    wait_for(recv_sems, 10, sums_all.at[:, pl.ds(0, cols_count - 1)])
    sums_ref[...] = sums_all[...]

    for slot, sent in ((0, dinput), (2, spectra), (4, parts), (5, result)):
        wait_for(send_sems, slot, sent.at[pl.ds(0, groups - 1)])
    wait_for(send_sems, 1, got_cols.at[pl.ds(0, cols_count - 1)])
    wait_for(send_sems, 3, got_rows.at[pl.ds(0, rows_count - 1)])
    wait_for(send_sems, 9, sums_rows.at[pl.ds(0, rows_count - 1)])
    wait_for(send_sems, 10, sums_all.at[:, pl.ds(0, cols_count - 1)])
    for slot, landed in halo_slots:
        wait_for(send_sems, slot, landed)


def finish_kernel(scaling, out_ref, sums_ref, data_ref, now_ref, past_ref, mix_ref, lift_ref):
    layer_count, channels = mix_ref.shape[:2]
    if data_ref.ndim == 2:
        small = out_ref.shape[2]
        for i in range(out_ref.shape[0]):
            data_ref[:, small * i : small * (i + 1)] = out_ref[i][:3]
    else:
        data_ref[...] = out_ref[...]
    sums = sums_ref[...].astype(F32) * scaling
    for layer in range(layer_count):
        first = 2 * channels * layer
        now_ref[layer] = sums[first : first + channels]
        past_ref[layer] = sums[first + channels : first + 2 * channels]
    first = 2 * channels * layer_count
    mix_ref[0] = sums[first : first + channels, :channels]
    mix_ref[1] = sums[first : first + channels, channels:]
    mix_ref[2] = sums[first + channels :, :channels]
    lift_ref[...] = sums[first + channels : first + channels + 3, channels:]


def constants(rows_count, cols_count, small):
    groups = rows_count * cols_count
    segment = groups * small
    ids = np.arange(groups)
    residues = ids // cols_count + rows_count * (ids % cols_count)
    unit = np.eye(4)
    swap = np.kron(np.eye(2), np.array([[0.0, -1.0], [1.0, 0.0]]))
    take = np.diag([1.0, 1.0, 1.0, 0.0])

    def blocks(left, right, sign, inner):
        angle = sign * 2.0 * np.pi / groups * (np.outer(left, right) % groups)
        return np.kron(np.cos(angle), unit @ inner) + np.kron(np.sin(angle), swap @ inner)

    turn_all = np.kron(np.eye(groups), swap)
    spread = blocks(residues, ids, -1.0, take)
    local = blocks(ids, ids, -1.0, unit)
    local_back = blocks(ids, ids, 1.0, unit)
    gather = np.kron(np.eye(groups), take) @ blocks(ids, residues, 1.0, unit)
    gather = gather / float(segment * groups)
    lanes = np.arange(small)
    angle = 2.0 * np.pi / small * (np.outer(lanes, lanes) % small)
    cosine, sine = np.cos(angle), np.sin(angle)
    fast = np.block([[cosine, sine], [-sine, cosine]])
    fast_back = np.block([[cosine, -sine], [sine, cosine]])
    angle = 2.0 * np.pi / segment * (np.outer(ids, lanes) % segment)
    angle = np.repeat(angle, 4, axis=0)
    twiddle = np.stack([np.cos(angle), np.sin(angle)]).astype(np.float32)
    return (
        residues,
        halves(np.concatenate([spread, turn_all @ spread])),
        halves(np.concatenate([local, turn_all @ local])),
        halves(fast),
        halves(fast_back),
        halves(local_back),
        halves(gather),
        twiddle,
    )


def turns(angle_steps, length, sign):
    angle = sign * 2.0 * math.pi / length * (angle_steps % length).astype(F32)
    return jnp.cos(angle), jnp.sin(angle)


def vmem():
    return pl.BlockSpec(memory_space=pltpu.VMEM)


def solution(mesh):
    rows_count, cols_count = mesh.shape["rows"], mesh.shape["cols"]
    groups = rows_count * cols_count

    def local(whitened, cotangent, lift, now, past, mix, dilations, psd_bin, psd_weight):
        segment = whitened.shape[1]
        layer_count, channels = mix.shape[:2]
        small = segment // groups
        length = segment * groups
        me = lax.axis_index("rows") * cols_count + lax.axis_index("cols")
        residue = lax.axis_index("rows") + rows_count * lax.axis_index("cols")
        _, spread, local_m, fast, fast_back, local_back, gather, twiddle = constants(
            rows_count, cols_count, small
        )
        samples = lax.broadcasted_iota(jnp.int32, (groups, small), 1)
        ids = lax.broadcasted_iota(jnp.int32, (groups, small), 0)
        residues = ids // cols_count + rows_count * (ids % cols_count)
        cos_a, sin_a = turns(residues * (me * small + samples), length, -1.0)
        cos_b, sin_b = turns(residue * (ids * small + samples), length, 1.0)

        wide = small == TILE
        bins = psd_bin.reshape(small, groups).T
        bins = jnp.tile(bins.reshape(-1, 1, TILE), (1, 4, 1)).reshape(-1, TILE)
        factor = pl.pallas_call(
            factors_kernel,
            out_shape=jax.ShapeDtypeStruct(bins.shape, F32),
            in_specs=[vmem()] * 2,
            out_specs=vmem(),
            name="factors",
        )(bins, psd_weight.reshape(-1, TILE))
        if not wide:
            factor = factor.reshape(-1, 4, TILE).transpose(1, 0, 2).reshape(4, groups, small)
            factor = factor.transpose(1, 0, 2).reshape(4 * groups, small)

        grad_rows = 2 * channels * (layer_count + 1)
        reach = segment + MARGIN
        cube = (groups, 4, small)
        share = (grad_rows // groups, 2 * channels)
        shares = (rows_count, cols_count) + share
        out, sums = pl.pallas_call(
            lambda *refs: whole_kernel(rows_count, cols_count, *refs),
            out_shape=(
                jax.ShapeDtypeStruct(cube, F32),
                jax.ShapeDtypeStruct(shares, BF16),
            ),
            in_specs=[vmem()] * 19,
            out_specs=(vmem(),) * 2,
            scratch_shapes=[
                pltpu.VMEM((3, reach + MARGIN), F32),
                pltpu.VMEM((channels, reach), BF16),
                pltpu.VMEM((2, channels, FRONT + MARGIN + reach), F32),
                pltpu.VMEM((layer_count, 3 * channels, reach), BF16),
                pltpu.VMEM((layer_count, 2 * channels, reach), F32),
                pltpu.VMEM((channels, reach), F32),
                pltpu.VMEM((2 * channels, reach + DMAX), BF16),
                pltpu.VMEM((3, MARGIN), F32),
                pltpu.VMEM((3, MARGIN), F32),
                pltpu.VMEM((channels, MARGIN), BF16),
                pltpu.VMEM(cube, F32),
                pltpu.VMEM(shares, BF16),
            ]
            + [pltpu.VMEM(cube, F32)] * 7
            + [
                pltpu.VMEM((cols_count, rows_count) + share, BF16),
                pltpu.VMEM((rows_count,) + share, F32),
                pltpu.VMEM((rows_count,) + share, F32),
                pltpu.VMEM(share, BF16),
                pltpu.VMEM((rows_count,) + share, BF16),
                pltpu.VMEM(shares, BF16),
                pltpu.SemaphoreType.DMA((11,)),
                pltpu.SemaphoreType.DMA((11,)),
            ],
            compiler_params=pltpu.CompilerParams(
                collective_id=0, has_side_effects=True, vmem_limit_bytes=60 * 2**20
            ),
            name="whole",
        )(
            jnp.broadcast_to(dilations[:, None], (layer_count, WIDE)), whitened, cotangent, lift.T, now.transpose(0, 2, 1),
            past.transpose(0, 2, 1), mix, factor, cos_a, sin_a, cos_b, sin_b, spread, local_m,
            fast, fast_back, local_back, gather, twiddle,
        )
        scaling = 1.0 / math.sqrt(float(length))
        data, now_t, past_t, mixes, lift_t = pl.pallas_call(
            lambda *refs: finish_kernel(scaling, *refs),
            out_shape=(
                jax.ShapeDtypeStruct((3, segment) if wide else cube, F32),
                jax.ShapeDtypeStruct((layer_count, channels, 2 * channels), F32),
                jax.ShapeDtypeStruct((layer_count, channels, 2 * channels), F32),
                jax.ShapeDtypeStruct((layer_count, channels, channels), F32),
                jax.ShapeDtypeStruct((3, channels), F32),
            ),
            in_specs=[vmem()] * 2,
            out_specs=(vmem(),) * 5,
            name="finish",
        )(out, sums.reshape(grad_rows, 2 * channels))
        if not wide:
            data = data.transpose(1, 0, 2).reshape(4, segment)[:3]
        return data, now_t.transpose(0, 2, 1), past_t.transpose(0, 2, 1), mixes, lift_t.T

    in_specs = (
        P(None, ("rows", "cols")),
        P(None, ("rows", "cols")),
        P(),
        P(),
        P(),
        P(),
        P(),
        P(None, "cols", "rows"),
        P(),
    )
    out_specs = (P(None, ("rows", "cols")), P(), P(), P(), P())
    return jax.shard_map(local, mesh=mesh, in_specs=in_specs, out_specs=out_specs, check_vma=False)
```

time: 66.5 us -> 57.6 us (0.87)
  local copies, waits for them, and re-layouts: 10.7 us -> 3.18 us
  starting transfers between devices: 4.92 us -> 0 us
  Pallas kernels: 46.2 us -> 51.1 us
  other arithmetic: 3.3 us -> 2.26 us
    unnamed x36 -> x7, local copies, waits for them, and re-layouts: 8.56 us -> 1.12 us
    pallas_call x2 -> x3, Pallas kernels: 46.2 us -> 51.1 us  [the longest x1 47.2 us: local(): pl.pallas_call(lambda *refs: whole_kernel(rows_count, cols_count, *refs),...]
    ppermute x3 -> x0, starting transfers between devices: 4.92 us -> none  [the longest x1 2.35 us: local(): left = lax.ppermute(whitened[:, segment - MARGIN:], both_axes, onward)]
    slice x5 -> x0, local copies, waits for them, and re-layouts: 1.83 us -> none  [the longest x1 0.9 us: local(): cot_right = lax.ppermute(cotangent[:, :MARGIN], both_axes, backward)]
    sin x0 -> x2, other arithmetic: none -> 1.55 us  [turns(): return (jnp.cos(angle), jnp.sin(angle))]
    another operation x2 -> x0, other arithmetic: 1.38 us -> none  [the longest x1 0.73 us: turns(): return jnp.stack([jnp.cos(angle), jnp.sin(angle)])]
    mul x2 -> x1, other arithmetic: 0.93 us -> 0.01 us  [local(): cos_b, sin_b = turns(residue * (ids * small + samples), length, 1.0)]
  transfers between devices with their start and end apart: 3 -> 0, of which waited for: 0 -> 0; matrix products, arithmetic and copies ran while one was open for 6% -> 0% of each run, Pallas kernels for 0% -> 0%
where the time goes in v1:
time: 57.6 us; the launch traced here: 57.3 us
  Pallas kernels  51.1 us (89%)
  local copies, waits for them, and re-layouts  3.18 us (6%)
  other arithmetic  2.26 us (4%)
  between operations  0.72 us (1%)
    pallas_call x1, Pallas kernels, local(): pl.pallas_call(lambda *refs: whole_kernel(rows_count, cols_count, *refs),...  47.2 us
    pallas_call x1, Pallas kernels, local(): pl.pallas_call(factors_kernel, out_shape=jax.ShapeDtypeStruct(bins.shape,...  2.26 us
    pallas_call x1, Pallas kernels, local(): pl.pallas_call(lambda *refs: finish_kernel(scaling, *refs), out_shape=(ja...  1.69 us
    sin x2, other arithmetic, turns(): return (jnp.cos(angle), jnp.sin(angle))  1.55 us

profile of v1, /device:TPU:0, one launch (start us, length us, event | category | flops | bytes accessed | tf_op | source)
XLA Modules:
  0.0 57.3 jit_solution(12357683890090409383)
XLA Ops:
  0.7 0.0 copy-start.2
  0.7 0.0 copy-start.1
  0.7 0.0 copy-start
  0.7 0.6 %copy-done.2 = s32[3]{0:T(128)S(1)} copy-done((s32[3]{0:T(128)S(1)}, s32[3]{0:T(128)}, u32[]{:S(2)}) %copy-start.2) | copy-done | bytes 36
  1.3 0.7 %broadcast_in_dim.2.refs_0_ = s32[3,256]{1,0:T(4,128)} broadcast(s32[3]{0:T(128)S(1)} %copy-done.2), dimensions={0} | broadcast | bytes 3084 | tf_op jit(solution)/shard_map/broadcast_in_dim | solution.py:529
  2.0 0.0 copy-done.1
  2.0 0.6 %reshape.25.psd_ref = f32[16,128]{1,0:T(8,128)} reshape(f32[2,1024]{1,0:T(2,128)S(1)} %copy-done.1) | data formatting | bytes 16384 | tf_op jit(solution)/shard_map/reshape | solution.py:481
  2.6 0.5 broadcast.63
  3.1 0.0 copy-done
  3.1 0.7 %reduce.3 = s32[4096]{0:T(1024)S(1)} reduce(s32[4096,1,1]{0,2,1:T(1,128)S(1)} %copy-done, s32[]{:T(128)} %broadcast.63), dimensions={1,2}, to_apply=%param.23.reduce_sub_computation.3 | reduce | bytes 32772 | tf_op args[7]
  3.8 0.8 %fusion.8 = (f32[32,128]{1,0:T(8,128)}, f32[32,128]{1,0:T(8,128)}) fusion(s32[128]{0:T(128)S(1)} %iota_add_fusion, s32[32]{0:T(128)S(1)} %get-tuple-element.26, s32[32]{0:T(128)S(1)} %get-tuple-element.27, pred[32]{0:T(512)(128)(4,1)S(1)} %get-tuple-element.23, s32[32]{0:T(128)S(1)} %get-tuple-element.25, s32[32]{0:T(128)S(1)} %get-tuple-element.28, ...), kind=kLoop, calls=%fused_computation.14 | loop fusion | flops 73728 | bytes 33856 | tf_op jit(solution)/shard_map/sin | solution.py:445
  4.6 0.8 %fusion.6 = (f32[32,128]{1,0:T(8,128)}, f32[32,128]{1,0:T(8,128)}) fusion(s32[32]{0:T(128)S(1)} %iota_multiply_fusion, s32[]{:T(128)S(6)} %add.42), kind=kLoop, calls=%fused_computation.12 | loop fusion | flops 61440 | bytes 32900 | tf_op jit(solution)/shard_map/sin | solution.py:445
  5.3 0.1 reshape.24
  5.4 0.1 copy.22
  5.5 0.7 %tile.7 = s32[32,4,128]{2,1,0:T(4,128)} broadcast(s32[32,128]{1,0:T(8,128)S(1)} %copy.22), dimensions={0,2} | broadcast | bytes 81920 | tf_op jit(solution)/shard_map/tile | solution.py:474
  6.2 2.3 %factors.1.refs_7_ = f32[128,128]{1,0:T(8,128)} custom-call(s32[128,128]{1,0:T(8,128)} %bitcast.11, f32[16,128]{1,0:T(8,128)} %reshape.25.psd_ref), custom_call_target="tpu_custom_call" | custom-call | tf_op jit(solution)/shard_map/factors/pallas_call | solution.py:475
  8.4 47.2 %whole.1 = (f32[32,4,128]{2,1,0:T(4,128)}, bf16[4,8,16,128]{3,2,1,0:T(8,128)(2,1)}) custom-call(s32[3,256]{1,0:T(4,128)} %broadcast_in_dim.2.refs_0_, f32[3,4096]{1,0:T(4,128)} %refs_1_.1, bf16[64,4096]{1,0:T(8,128)(2,1)} %refs_2_.1, f32[3,64]{1,0:T(4,128)} %bitcast.15, bf16[3,64,128]{2,1,0:T(8,128)(2,1)} %bitcast.13, bf16[3,64,128]{2,1,0:T(8,128)(2,1)} %bitcast.14, ...), custom_call_target="tpu_custom_call" | custom-call | tf_op jit(solution)/shard_map/whole/pallas_call | solution.py:491
  55.6 1.7 %finish.1 = (f32[3,4096]{1,0:T(4,128)}, f32[3,64,128]{2,1,0:T(8,128)}, f32[3,64,128]{2,1,0:T(8,128)}, f32[3,64,64]{2,1,0:T(8,128)}, f32[3,64]{1,0:T(4,128)}) custom-call(f32[32,4,128]{2,1,0:T(4,128)} %get-tuple-element.12.refs_0_, bf16[512,128]{1,0:T(8,128)(2,1)} %bitcast.12), custom_call_target="tpu_custom_call" | custom-call | tf_op jit(solution)/shard_map/finish/pallas_call | solution.py:534
  (5 shorter events, 0.0 us)
Async XLA Ops:
  0.7 0.7 %copy-start.2 = (s32[3]{0:T(128)S(1)}, s32[3]{0:T(128)}, u32[]{:S(2)}) copy-start(s32[3]{0:T(128)} %param.22) | copy-start | bytes 40
  0.7 1.3 %copy-start.1 = (f32[2,1024]{1,0:T(2,128)S(1)}, f32[2,1024]{1,0:T(2,128)}, u32[]{:S(2)}) copy-start(f32[2,1024]{1,0:T(2,128)} %param.24) | copy-start | bytes 24580
  0.7 2.4 %copy-start = (s32[4096,1,1]{0,2,1:T(1,128)S(1)}, s32[4096,1,1]{0,2,1:T(1,128)}, u32[]{:S(2)}) copy-start(s32[4096,1,1]{0,2,1:T(1,128)} %param.23) | copy-start | bytes 49156

commit v2 on v1

--- a/solution.py
+++ b/solution.py
@@ -47,23 +47,50 @@
     return list(zip(cuts[:-1], cuts[1:]))
 
 
-def factors_kernel(bins_ref, psd_ref, factor_ref):
+def turns(angle_steps, length, sign):
+    angle = sign * 2.0 * math.pi / length * lax.rem(angle_steps, length).astype(F32)
+    return jnp.cos(angle), jnp.sin(angle)
+
+
+def prepare_kernel(
+    rows_count, cols_count, length,
+    dil_ref, bins_ref, psd_ref,
+    factor_ref, cos_a_ref, sin_a_ref, cos_b_ref, sin_b_ref, delays_ref,
+):
     bins = bins_ref[...]
-    table_rows = psd_ref.shape[0] // 2
-    row_at = lax.broadcasted_iota(jnp.int32, bins.shape, 0)
-    first_row = jnp.where(lax.rem(row_at, 4) < 2, 0, table_rows)
-    entry_row = lax.shift_right_logical(bins, 7) + first_row
+    entry_row = lax.shift_right_logical(bins, 7)
     entry_lane = jnp.bitwise_and(bins, TILE - 1)
-    factor = jnp.zeros(bins.shape, F32)
-    for row in range(2 * table_rows):
-        table = jnp.broadcast_to(psd_ref[row : row + 1, :], (bins.shape[0], TILE))
-        found = jnp.take_along_axis(table, entry_lane, axis=1)
-        factor = jnp.where(entry_row == row, found, factor)
-    factor_ref[...] = factor
+    factors = []
+    for kind in range(2):
+        factor = jnp.zeros(bins.shape, F32)
+        for row in range(psd_ref.shape[1] // TILE):
+            table = psd_ref[kind : kind + 1, TILE * row : TILE * (row + 1)]
+            table = jnp.broadcast_to(table, bins.shape)
+            found = jnp.take_along_axis(table, entry_lane, axis=1)
+            factor = jnp.where(entry_row == row, found, factor)
+        factors.append(factor)
+    signal = lax.broadcasted_iota(jnp.int32, (bins.shape[0], 4, TILE), 1)
+    factor_ref[...] = jnp.where(
+        signal < 2, factors[0][:, None, :], factors[1][:, None, :]
+    ).reshape(factor_ref.shape)
+
+    shape = cos_a_ref.shape
+    groups, small = shape
+    my_row, my_col = lax.axis_index("rows"), lax.axis_index("cols")
+    me = my_row * cols_count + my_col
+    residue = my_row + rows_count * my_col
+    samples = lax.broadcasted_iota(jnp.int32, shape, 1)
+    ids = lax.broadcasted_iota(jnp.int32, shape, 0)
+    rows = sum((ids >= cols_count * i).astype(jnp.int32) for i in range(1, rows_count))
+    residues = rows + rows_count * (ids - cols_count * rows)
+    cos_a_ref[...], sin_a_ref[...] = turns(residues * (me * small + samples), length, -1.0)
+    cos_b_ref[...], sin_b_ref[...] = turns(residue * (ids * small + samples), length, 1.0)
+    for layer in range(dil_ref.shape[0]):
+        delays_ref[layer : layer + 1, :] = jnp.full((1, WIDE), dil_ref[layer], jnp.int32)
 
 
 def layers(
-    before_halos, halos,
+    before_halos, halos, leave,
     dil_ref, white_ref, cot_ref, lift_ref, now_ref, past_ref, mix_ref,
     dinput_ref, grads_ref, inputs, cot, field, seen, gates, dfield, ahead,
 ):
@@ -154,16 +181,15 @@
                 gates[layer, 0:channels, start:stop] = filt
                 gates[layer, channels:, start:stop] = sig
 
-    taps, mixes = [], []
-    ahead[...] = jnp.zeros(ahead.shape, BF16)
+    small = dinput_ref.shape[2]
     for layer in reversed(range(layer_count)):
         delays = dil_ref[layer : layer + 1, :]
         matrix = picks(delays)
         weight_t = jnp.concatenate([now_ref[layer], past_ref[layer]], axis=1)
         mix_t = mix_ref[layer].T
-        reach = min(MARGIN, DMAX * (layer + 1))
-        total = jnp.zeros((3 * channels, 3 * channels), F32)
-        for start, stop in reversed(chunks_of(0, segment + reach)):
+        reach = segment + min(MARGIN, DMAX * (layer + 1))
+        ahead[layer, 0 : 2 * channels, reach : reach + DMAX] = jnp.zeros((2 * channels, DMAX), BF16)
+        for start, stop in reversed(chunks_of(0, reach)):
             size = stop - start
             if layer == layer_count - 1:
                 grad_b = cot[:, start:stop]
@@ -178,31 +204,44 @@
             dpre = jnp.concatenate(
                 [dgate_sig * (1.0 - filt * filt), dgate_sig * filt * (1.0 - sig)], axis=0
             ).astype(BF16)
-            ahead[:, start:stop] = dpre
-            later = moved(ahead[:, start : stop + DMAX], matrix)
-            dfield[:, start:stop] = grad + jnp.dot(
+            ahead[layer, 0 : 2 * channels, start:stop] = dpre
+            later = moved(ahead[layer, 0 : 2 * channels, start : stop + DMAX], matrix)
+            if start < segment:
+                ahead[layer, 2 * channels :, start:stop] = grad_b
+            grad = grad + jnp.dot(
                 weight_t, jnp.concatenate([dpre, later], axis=0), preferred_element_type=F32
             )
-            if start < segment:
-                left = jnp.concatenate([dpre, grad_b], axis=0)
-                total += lax.dot_general(
-                    seen[layer, :, start:stop], left, (((1,), (1,)), ((), ())),
-                    preferred_element_type=F32,
-                )
-        taps.insert(0, total[: 2 * channels, : 2 * channels])
-        mixes.insert(0, total[2 * channels :, 2 * channels :].T)
-
+            dfield[:, start:stop] = grad
+            if layer > 0 or start >= segment:
+                continue
+            part = jnp.dot(
+                lift_t, grad, preferred_element_type=F32, precision=lax.Precision.HIGHEST
+            )
+            part = jnp.concatenate([part, jnp.zeros((1, size), F32)], axis=0)
+            for i in range(size // small):
+                dinput_ref[start // small + i] = part[:, small * i : small * (i + 1)]
+            for i in range(size // small):
+                leave(start // small + i)
+
+
+def weight_sums(mix_ref, grads_ref, inputs, seen, dfield, ahead):
+    layer_count, channels = mix_ref.shape[:2]
+    segment = seen.shape[2] - MARGIN
+    taps, mixes = [], []
+    for layer in range(layer_count):
+        total = jnp.zeros((3 * channels, 3 * channels), F32)
+        for start, stop in chunks_of(0, segment):
+            total += lax.dot_general(
+                seen[layer, :, start:stop], ahead[layer, :, start:stop],
+                (((1,), (1,)), ((), ())), preferred_element_type=F32,
+            )
+        taps.append(total[: 2 * channels, : 2 * channels])
+        mixes.append(total[2 * channels :, 2 * channels :].T)
     lift_total = jnp.zeros((3, channels), F32)
     for start, stop in chunks_of(0, segment):
-        grad = dfield[:, start:stop]
-        x = inputs[:, at(start) : at(stop)]
-        part = jnp.dot(lift_t, grad, preferred_element_type=F32, precision=lax.Precision.HIGHEST)
-        part = jnp.concatenate([part, jnp.zeros((1, stop - start), F32)], axis=0)
-        small = dinput_ref.shape[2]
-        for i in range((stop - start) // small):
-            dinput_ref[start // small + i] = part[:, small * i : small * (i + 1)]
         lift_total += lax.dot_general(
-            x, grad, (((1,), (1,)), ((), ())), preferred_element_type=F32,
+            inputs[:, MARGIN + start : MARGIN + stop], dfield[:, start:stop],
+            (((1,), (1,)), ((), ())), preferred_element_type=F32,
             precision=lax.Precision.HIGHEST,
         )
     lift_block = jnp.concatenate([lift_total, jnp.zeros((channels - 3, channels), F32)], axis=0)
@@ -299,8 +338,14 @@
         cot_right = jnp.where(me == groups - 1, 0.0, cot_halo[...].astype(F32)).astype(BF16)
         return left, right, cot_right
 
+    def leave(block):
+        @pl.when(me != block)
+        def _():
+            row, col = block // cols_count, block % cols_count
+            send(0, dinput.at[block], got_x.at[me], row, col)
+
     layers(
-        before_halos, halos,
+        before_halos, halos, leave,
         dil_ref, white_ref, cot_ref, lift_ref, now_ref, past_ref, mix_ref,
         dinput, grads, inputs, cot, field, seen, gates, dfield, ahead,
     )
@@ -314,7 +359,8 @@
         sine = jnp.broadcast_to(sin_ref[...][:, None, :], cube).reshape(flat)
         return (here * cosine + turned * sine).reshape(cube)
 
-    exchange(0, dinput, got_x)
+    got_x[me] = dinput[me]
+    weight_sums(mix_ref, grads, inputs, seen, dfield, ahead)
     for col in cols[1:]:
         send(1, grads.at[:, col], got_cols.at[my_col], my_row, col)
     got_cols[my_col] = grads[:, my_col]
@@ -440,11 +486,6 @@
     )
 
 
-def turns(angle_steps, length, sign):
-    angle = sign * 2.0 * math.pi / length * (angle_steps % length).astype(F32)
-    return jnp.cos(angle), jnp.sin(angle)
-
-
 def vmem():
     return pl.BlockSpec(memory_space=pltpu.VMEM)
 
@@ -458,27 +499,20 @@
         layer_count, channels = mix.shape[:2]
         small = segment // groups
         length = segment * groups
-        me = lax.axis_index("rows") * cols_count + lax.axis_index("cols")
-        residue = lax.axis_index("rows") + rows_count * lax.axis_index("cols")
         _, spread, local_m, fast, fast_back, local_back, gather, twiddle = constants(
             rows_count, cols_count, small
         )
-        samples = lax.broadcasted_iota(jnp.int32, (groups, small), 1)
-        ids = lax.broadcasted_iota(jnp.int32, (groups, small), 0)
-        residues = ids // cols_count + rows_count * (ids % cols_count)
-        cos_a, sin_a = turns(residues * (me * small + samples), length, -1.0)
-        cos_b, sin_b = turns(residue * (ids * small + samples), length, 1.0)
-
         wide = small == TILE
-        bins = psd_bin.reshape(small, groups).T
-        bins = jnp.tile(bins.reshape(-1, 1, TILE), (1, 4, 1)).reshape(-1, TILE)
-        factor = pl.pallas_call(
-            factors_kernel,
-            out_shape=jax.ShapeDtypeStruct(bins.shape, F32),
-            in_specs=[vmem()] * 2,
-            out_specs=vmem(),
-            name="factors",
-        )(bins, psd_weight.reshape(-1, TILE))
+        bins = psd_bin.reshape(small, groups).T.reshape(-1, TILE)
+        factor, cos_a, sin_a, cos_b, sin_b, delays = pl.pallas_call(
+            lambda *refs: prepare_kernel(rows_count, cols_count, length, *refs),
+            out_shape=(jax.ShapeDtypeStruct((4 * bins.shape[0], TILE), F32),)
+            + (jax.ShapeDtypeStruct((groups, small), F32),) * 4
+            + (jax.ShapeDtypeStruct((layer_count, WIDE), jnp.int32),),
+            in_specs=[pl.BlockSpec(memory_space=pltpu.SMEM)] + [vmem()] * 2,
+            out_specs=(vmem(),) * 6,
+            name="prepare",
+        )(dilations, bins, psd_weight)
         if not wide:
             factor = factor.reshape(-1, 4, TILE).transpose(1, 0, 2).reshape(4, groups, small)
             factor = factor.transpose(1, 0, 2).reshape(4 * groups, small)
@@ -503,7 +537,7 @@
                 pltpu.VMEM((layer_count, 3 * channels, reach), BF16),
                 pltpu.VMEM((layer_count, 2 * channels, reach), F32),
                 pltpu.VMEM((channels, reach), F32),
-                pltpu.VMEM((2 * channels, reach + DMAX), BF16),
+                pltpu.VMEM((layer_count, 3 * channels, reach + DMAX), BF16),
                 pltpu.VMEM((3, MARGIN), F32),
                 pltpu.VMEM((3, MARGIN), F32),
                 pltpu.VMEM((channels, MARGIN), BF16),
@@ -526,7 +560,7 @@
             ),
             name="whole",
         )(
-            jnp.broadcast_to(dilations[:, None], (layer_count, WIDE)), whitened, cotangent, lift.T, now.transpose(0, 2, 1),
+            delays, whitened, cotangent, lift.T, now.transpose(0, 2, 1),
             past.transpose(0, 2, 1), mix, factor, cos_a, sin_a, cos_b, sin_b, spread, local_m,
             fast, fast_back, local_back, gather, twiddle,
         )

time: 57.6 us -> 53.7 us (0.932)
  local copies, waits for them, and re-layouts: 3.18 us -> 1.27 us
  Pallas kernels: 51.1 us -> 50.1 us
  other arithmetic: 2.26 us -> 1.4 us
    sin x2 -> x0, other arithmetic: 1.55 us -> none  [turns(): return (jnp.cos(angle), jnp.sin(angle))]
    unnamed x1, other arithmetic: 0.68 us -> 1.4 us
    another operation x1 -> x0, local copies, waits for them, and re-layouts: 0.67 us -> none  [local(): bins = jnp.tile(bins.reshape(-1, 1, TILE), (1, 4, 1)).reshape(-1, TILE)]
    broadcast_in_dim x1 -> x0, local copies, waits for them, and re-layouts: 0.65 us -> none  [local(): jnp.broadcast_to(dilations[:, None], (layer_count, WIDE))]
    unnamed x7 -> x1, local copies, waits for them, and re-layouts: 1.12 us -> 0.51 us
    pallas_call x1, Pallas kernels: 2.26 us -> 1.66 us  [local(): pl.pallas_call(lambda *refs: prepare_kernel(rows_count, cols_count, lengt...]
where the time goes in v2:
time: 53.7 us; the launch traced here: 53.4 us
  Pallas kernels  50.1 us (93%)
  other arithmetic  1.4 us (3%)
  local copies, waits for them, and re-layouts  1.27 us (2%)
  between operations  0.64 us (1%)
    pallas_call x1, Pallas kernels, local(): pl.pallas_call(lambda *refs: whole_kernel(rows_count, cols_count, *refs),...  46.7 us
    pallas_call x1, Pallas kernels, local(): pl.pallas_call(lambda *refs: finish_kernel(scaling, *refs), out_shape=(ja...  1.69 us
    pallas_call x1, Pallas kernels, local(): pl.pallas_call(lambda *refs: prepare_kernel(rows_count, cols_count, lengt...  1.66 us
    unnamed x1, other arithmetic  1.4 us

profile of v2, /device:TPU:0, one launch (start us, length us, event | category | flops | bytes accessed | tf_op | source)
XLA Modules:
  0.0 53.4 jit_solution(3770606548181714850)
XLA Ops:
  0.6 0.5 broadcast.3
  1.1 1.4 %reduce.3 = s32[4096]{0:T(1024)S(1)} reduce(s32[4096,1,1]{0,2,1:T(1,128)} %param.23, s32[]{:T(128)} %broadcast.3), dimensions={1,2}, to_apply=%param.23.reduce_sub_computation.3 | reduce | bytes 32772 | tf_op args[7]
  2.5 0.1 reshape.16
  2.6 0.7 %copy.21 = s32[128,32]{0,1:T(8,128)} copy(s32[128,32]{1,0:T(8,128)S(1)} %reshape.16) | data formatting | bytes 32768 | tf_op jit(solution)/shard_map/reshape | solution.py:506
  3.3 1.7 %prepare.1 = (f32[128,128]{1,0:T(8,128)}, f32[32,128]{1,0:T(8,128)}, f32[32,128]{1,0:T(8,128)}, f32[32,128]{1,0:T(8,128)}, f32[32,128]{1,0:T(8,128)}, /*index=5*/s32[3,256]{1,0:T(4,128)}) custom-call(s32[3]{0:T(128)} %refs_0_.1, s32[32,128]{1,0:T(8,128)} %bitcast.10, f32[2,1024]{1,0:T(2,128)} %refs_2_.2), custom_call_target="tpu_custom_call" | custom-call | tf_op jit(solution)/shard_map/prepare/pallas_call | solution.py:507
  5.0 46.7 %whole.1 = (f32[32,4,128]{2,1,0:T(4,128)}, bf16[4,8,16,128]{3,2,1,0:T(8,128)(2,1)}) custom-call(s32[3,256]{1,0:T(4,128)} %get-tuple-element.18.refs_0_, f32[3,4096]{1,0:T(4,128)} %refs_1_.1, bf16[64,4096]{1,0:T(8,128)(2,1)} %refs_2_.3, f32[3,64]{1,0:T(4,128)} %bitcast.13, bf16[3,64,128]{2,1,0:T(8,128)(2,1)} %bitcast.11, bf16[3,64,128]{2,1,0:T(8,128)(2,1)} %bitcast.12, ...), custom_call_target="tpu_custom_call" | custom-call | tf_op jit(solution)/shard_map/whole/pallas_call | solution.py:525
  51.7 1.7 %finish.1 = (f32[3,4096]{1,0:T(4,128)}, f32[3,64,128]{2,1,0:T(8,128)}, f32[3,64,128]{2,1,0:T(8,128)}, f32[3,64,64]{2,1,0:T(8,128)}, f32[3,64]{1,0:T(4,128)}) custom-call(f32[32,4,128]{2,1,0:T(4,128)} %get-tuple-element.24.refs_0_, bf16[512,128]{1,0:T(8,128)(2,1)} %bitcast.9), custom_call_target="tpu_custom_call" | custom-call | tf_op jit(solution)/shard_map/finish/pallas_call | solution.py:568

commit v3 on v2

--- a/solution.py
+++ b/solution.py
@@ -57,7 +57,13 @@
     dil_ref, bins_ref, psd_ref,
     factor_ref, cos_a_ref, sin_a_ref, cos_b_ref, sin_b_ref, delays_ref,
 ):
-    bins = bins_ref[...]
+    if bins_ref.ndim == 3:
+        rows = bins_ref.shape[2] // TILE
+        bins = jnp.concatenate(
+            [bins_ref[0, :, TILE * i : TILE * (i + 1)] for i in range(rows)], axis=0
+        )
+    else:
+        bins = bins_ref[...]
     entry_row = lax.shift_right_logical(bins, 7)
     entry_lane = jnp.bitwise_and(bins, TILE - 1)
     factors = []
@@ -68,6 +74,11 @@
             table = jnp.broadcast_to(table, bins.shape)
             found = jnp.take_along_axis(table, entry_lane, axis=1)
             factor = jnp.where(entry_row == row, found, factor)
+        if bins_ref.ndim == 3:
+            turned = factor.T
+            factor = jnp.concatenate(
+                [turned[i : i + rows] for i in range(0, TILE, rows)], axis=1
+            )
         factors.append(factor)
     signal = lax.broadcasted_iota(jnp.int32, (bins.shape[0], 4, TILE), 1)
     factor_ref[...] = jnp.where(
@@ -380,6 +391,16 @@
     got_rows[my_row] = part_sums[my_row]
 
     wait_for(recv_sems, 2, got_spectra.at[pl.ds(0, groups - 1)])
+
+    wait_for(recv_sems, 3, got_rows.at[pl.ds(0, rows_count - 1)])
+    total = got_rows[0]
+    for i in range(1, rows_count):
+        total += got_rows[i]
+    own_sum[...] = total.astype(BF16)
+    for row in rows[1:]:
+        send(9, own_sum, sums_rows.at[my_row], row, my_col)
+    sums_rows[my_row] = own_sum[...]
+
     both = dot_left(local_ref, got_spectra[...].reshape(flat))
     here, turned = both[: 4 * groups], both[4 * groups :]
     cosine, sine = twiddle_ref[0], twiddle_ref[1]
@@ -394,23 +415,14 @@
     parts[...] = turned_by((pair[:, :small], pair[:, small:]), cos_b_ref, sin_b_ref)
     exchange(4, parts, got_parts)
 
-    wait_for(recv_sems, 3, got_rows.at[pl.ds(0, rows_count - 1)])
-    total = got_rows[0]
-    for i in range(1, rows_count):
-        total += got_rows[i]
-    own_sum[...] = total.astype(BF16)
-    for row in rows[1:]:
-        send(9, own_sum, sums_rows.at[my_row], row, my_col)
-    sums_rows[my_row] = own_sum[...]
-
-    wait_for(recv_sems, 4, got_parts.at[pl.ds(0, groups - 1)])
-    result[...] = dot_left(gather_ref, got_parts[...].reshape(flat)).reshape(cube)
-    exchange(5, result, got_result)
-
     wait_for(recv_sems, 9, sums_rows.at[pl.ds(0, rows_count - 1)])
     for col in cols[1:]:
         send(10, sums_rows, sums_all.at[:, my_col], my_row, col)
     sums_all[:, my_col] = sums_rows[...]
+
+    wait_for(recv_sems, 4, got_parts.at[pl.ds(0, groups - 1)])
+    result[...] = dot_left(gather_ref, got_parts[...].reshape(flat)).reshape(cube)
+    exchange(5, result, got_result)
 
     wait_for(recv_sems, 5, got_result.at[pl.ds(0, groups - 1)])
     out_ref[...] = got_result[...]
@@ -467,10 +479,13 @@
     gather = np.kron(np.eye(groups), take) @ blocks(ids, residues, 1.0, unit)
     gather = gather / float(segment * groups)
     lanes = np.arange(small)
-    angle = 2.0 * np.pi / small * (np.outer(lanes, lanes) % small)
+    order = lanes
+    if small == TILE:
+        order = lanes.reshape(groups, small // groups).T.reshape(-1)
+    angle = 2.0 * np.pi / small * (np.outer(lanes, order) % small)
     cosine, sine = np.cos(angle), np.sin(angle)
     fast = np.block([[cosine, sine], [-sine, cosine]])
-    fast_back = np.block([[cosine, -sine], [sine, cosine]])
+    fast_back = np.block([[cosine.T, -sine.T], [sine.T, cosine.T]])
     angle = 2.0 * np.pi / segment * (np.outer(ids, lanes) % segment)
     angle = np.repeat(angle, 4, axis=0)
     twiddle = np.stack([np.cos(angle), np.sin(angle)]).astype(np.float32)
@@ -503,10 +518,13 @@
             rows_count, cols_count, small
         )
         wide = small == TILE
-        bins = psd_bin.reshape(small, groups).T.reshape(-1, TILE)
+        if wide:
+            bins = psd_bin.transpose(1, 2, 0)
+        else:
+            bins = psd_bin.reshape(small, groups).T.reshape(-1, TILE)
         factor, cos_a, sin_a, cos_b, sin_b, delays = pl.pallas_call(
             lambda *refs: prepare_kernel(rows_count, cols_count, length, *refs),
-            out_shape=(jax.ShapeDtypeStruct((4 * bins.shape[0], TILE), F32),)
+            out_shape=(jax.ShapeDtypeStruct((4 * (segment // TILE), TILE), F32),)
             + (jax.ShapeDtypeStruct((groups, small), F32),) * 4
             + (jax.ShapeDtypeStruct((layer_count, WIDE), jnp.int32),),
             in_specs=[pl.BlockSpec(memory_space=pltpu.SMEM)] + [vmem()] * 2,

time: 53.7 us -> 52 us (0.968)
  other arithmetic: 1.4 us -> 0 us
  local copies, waits for them, and re-layouts: 1.27 us -> 0 us
  Pallas kernels: 50.1 us -> 51.1 us
    unnamed x1 -> x0, other arithmetic: 1.4 us -> none
    pallas_call x1, Pallas kernels: 46.7 us -> 47.5 us  [local(): pl.pallas_call(lambda *refs: whole_kernel(rows_count, cols_count, *refs),...]
    reshape x2 -> x0, local copies, waits for them, and re-layouts: 0.76 us -> none  [local(): bins = psd_bin.reshape(small, groups).T.reshape(-1, TILE)]
where the time goes in v3:
time: 52 us; the launch traced here: 51.7 us
  Pallas kernels  51.1 us (98%)
  between operations  0.64 us (1%)
    pallas_call x1, Pallas kernels, local(): pl.pallas_call(lambda *refs: whole_kernel(rows_count, cols_count, *refs),...  47.5 us
    pallas_call x1, Pallas kernels, local(): pl.pallas_call(lambda *refs: prepare_kernel(rows_count, cols_count, lengt...  1.9 us
    pallas_call x1, Pallas kernels, local(): pl.pallas_call(lambda *refs: finish_kernel(scaling, *refs), out_shape=(ja...  1.69 us

profile of v3, /device:TPU:0, one launch (start us, length us, event | category | flops | bytes accessed | tf_op | source)
XLA Modules:
  0.0 51.7 jit_solution(9659694982964886856)
XLA Ops:
  0.6 1.9 %prepare.1 = (f32[128,128]{1,0:T(8,128)}, f32[32,128]{1,0:T(8,128)}, f32[32,128]{1,0:T(8,128)}, f32[32,128]{1,0:T(8,128)}, f32[32,128]{1,0:T(8,128)}, /*index=5*/s32[3,256]{1,0:T(4,128)}) custom-call(s32[3]{0:T(128)} %refs_0_.1, s32[1,1,4096]{2,1,0:T(1,128)} %bitcast.11, f32[2,1024]{1,0:T(2,128)} %refs_2_.2), custom_call_target="tpu_custom_call" | custom-call | tf_op jit(solution)/shard_map/prepare/pallas_call | solution.py:525
  2.5 47.5 %whole.1 = (f32[32,4,128]{2,1,0:T(4,128)}, bf16[4,8,16,128]{3,2,1,0:T(8,128)(2,1)}) custom-call(s32[3,256]{1,0:T(4,128)} %get-tuple-element.18.refs_0_, f32[3,4096]{1,0:T(4,128)} %refs_1_.1, bf16[64,4096]{1,0:T(8,128)(2,1)} %refs_2_.3, f32[3,64]{1,0:T(4,128)} %bitcast.12, bf16[3,64,128]{2,1,0:T(8,128)(2,1)} %bitcast.9, bf16[3,64,128]{2,1,0:T(8,128)(2,1)} %bitcast.10, ...), custom_call_target="tpu_custom_call" | custom-call | tf_op jit(solution)/shard_map/whole/pallas_call | solution.py:543
  50.1 1.7 %finish.1 = (f32[3,4096]{1,0:T(4,128)}, f32[3,64,128]{2,1,0:T(8,128)}, f32[3,64,128]{2,1,0:T(8,128)}, f32[3,64,64]{2,1,0:T(8,128)}, f32[3,64]{1,0:T(4,128)}) custom-call(f32[32,4,128]{2,1,0:T(4,128)} %get-tuple-element.24.refs_0_, bf16[512,128]{1,0:T(8,128)(2,1)} %bitcast.8), custom_call_target="tpu_custom_call" | custom-call | tf_op jit(solution)/shard_map/finish/pallas_call | solution.py:586
